TPU v7x, 512 devices: a whole 4x8x8 slice. The times are simulated.
512 devices in a mesh: seq: 32 (over y, x), head: 16 (over z, core).
Axes of the slice: x: 4, y: 8, z: 8, core: 2. Of those that a mesh axis runs over, the one named last changes fastest.
Arguments:
- queries: bfloat16 [65536, 128], P('seq', 'head'), may hold values from -0.1875 to 0.1875
- key_vectors: bfloat16 [65536, 128], P('seq', 'head'), may hold values from -0.1875 to 0.1875
- values: bfloat16 [65536, 4096], P('seq', 'head'), may hold values from -6 to 6
- level_table: float32 [8, 17], replicated, may hold values from 0.25 to 2.5
- level_class: int32 [65536], P('seq'), may hold values from 0 to 7
- doc_ids: int32 [65536], P('seq'), may hold values from 0 to 2, never falling along the last dimension, each value on 1 to 33792 neighbouring positions
Outputs:
- mixed: bfloat16 [65536, 4096], P('seq', 'head')
Inputs may be any that keep to these rules, and one draw needn't show every extreme that they name: `doc_ids`: document numbers never fall along the window; each document is one run of tokens, the longest exactly 33792 tokens.
All inputs are finite; a program needn't handle non-finite values.
Results may differ from a plain program's by a relative error of at most 0.013.
Values may be sent and summed in bfloat16 or wider, within the bound.
A program may use at most 64 MiB of HBM per device.

v0:
```python
import jax
import jax.numpy as jnp
from jax import lax
from jax.experimental import pallas as pl
from jax.experimental.pallas import tpu as pltpu
from jax.sharding import PartitionSpec as P

MESH = pl.DeviceIdType.MESH
F32 = jnp.float32
BF16 = jnp.bfloat16

X = 4
Y = 8
Z = 8
TILE = 256
NT = 8
HALF = 128
WIDTH = 256
NEAR_LEVELS = 9
MID_LEVELS = 3
FAR_LEVELS = 5
QROWS = 32
TAGGED = QROWS + 16
Z_ORDER = (4, 3, 5, 2, 6, 1, 7)
DIM0 = (((0,), (0,)), ((), ()))


def dot(a, b):
    return jnp.dot(a, b, preferred_element_type=F32)


def same(a, b):
    return jnp.where(a == b, 1.0, 0.0).astype(F32)


def body(
    k_hbm,
    q_hbm,
    v_hbm,
    tab_ref,
    cls_ref,
    doc_ref,
    out_ref,
    k8,
    q8,
    v,
    kg,
    qg,
    onehot,
    table,
    grid,
    kt,
    state,
    left9,
    left10,
    left11,
    tails,
    xbuf,
    xlow,
    xout,
    ysend,
    ybuf,
    ylow,
    yout,
    ymask,
    bucket,
    qw,
    near,
    in_sem,
    ks_sem,
    kr_sem,
    kps_sem,
    kpr_sem,
    qs_sem,
    qr_sem,
    qps_sem,
    qpr_sem,
    xs_sem,
    xr_sem,
    as_sem,
    ar_sem,
    ys_sem,
    yr_sem,
    bs_sem,
    br_sem,
):
    seq = lax.axis_index("seq")
    head = lax.axis_index("head")
    x = seq % X
    y = seq // X
    z = head // 2
    c = head % 2

    def at_z(d):
        return {"seq": seq, "head": ((z + d) % Z) * 2 + c}

    def at_x(d):
        return {"seq": y * X + (x + d) % X, "head": head}

    def at_y(row):
        return {"seq": row * X + x, "head": head}

    partner = {"seq": seq, "head": z * 2 + (1 - c)}

    def remote(src, dst, send, recv, device):
        return pltpu.make_async_remote_copy(
            src_ref=src,
            dst_ref=dst,
            send_sem=send,
            recv_sem=recv,
            device_id=device,
            device_id_type=MESH,
        )

    load_k = pltpu.make_async_copy(k_hbm, k8, in_sem.at[0])
    load_q = pltpu.make_async_copy(q_hbm, q8, in_sem.at[1])
    load_v = pltpu.make_async_copy(v_hbm, v, in_sem.at[2])
    load_k.start()
    load_q.start()
    load_v.start()

    barrier = pltpu.get_barrier_semaphore()
    peers = [at_z(d) for d in range(1, Z)] + [at_x(d) for d in range(1, X)]
    peers = peers + [at_y((y + d) % Y) for d in range(1, Y)] + [partner]
    for peer in peers:
        pl.semaphore_signal(barrier, inc=1, device_id=peer, device_id_type=MESH)

    def pack(shard):
        wide = shard[...].astype(F32)
        return jnp.concatenate([wide[:, :1024], wide[:, 1024:]], axis=0).astype(BF16)

    load_k.wait()
    kg[c, z] = pack(k8)
    load_q.wait()
    qg[c, z] = pack(q8)
    pl.semaphore_wait(barrier, len(peers))

    k_copies = {}
    q_copies = {}
    for d in Z_ORDER:
        k_copies[d] = remote(kg.at[c, z], kg.at[c, z], ks_sem.at[d], kr_sem.at[d], at_z(d))
        k_copies[d].start()

    def k_partner(d):
        slot = kg.at[c, (z + Z - d) % Z]
        return remote(slot, slot, kps_sem.at[d], kpr_sem.at[d], partner)

    k_partner(0).start()
    for d in Z_ORDER:
        q_copies[d] = remote(qg.at[c, z], qg.at[c, z], qs_sem.at[d], qr_sem.at[d], at_z(d))
        q_copies[d].start()

    for order, level in enumerate(list(range(NEAR_LEVELS)) + [None] + list(range(NEAR_LEVELS, 17))):
        columns = slice(order * HALF, (order + 1) * HALF)
        if level is None:
            row = lax.broadcasted_iota(jnp.int32, (32, HALF), 0)
            table[:, columns] = jnp.where(row == 24, 1.0, 0.0).astype(BF16)
        else:
            weight = jnp.broadcast_to(tab_ref[:, level : level + 1], (8, HALF))
            high = weight.astype(BF16).astype(F32)
            middle = (weight - high).astype(BF16).astype(F32)
            low = weight - high - middle
            parts = [high, middle, low, jnp.zeros_like(low)]
            table[:, columns] = jnp.concatenate(parts, axis=0).astype(BF16)

    def doc_row(block):
        return doc_ref[pl.ds(block, 1), :].astype(F32)

    def doc_tile(i):
        return jnp.concatenate([doc_row(2 * i), doc_row(2 * i + 1)], axis=1)

    first_doc = doc_ref[0:1, 0:1].astype(F32)

    def last_doc(i):
        return doc_ref[2 * i + 1 : 2 * i + 2, HALF - 1 : HALF].astype(F32)

    @pl.loop(0, NT)
    def _(i):
        row8 = lax.broadcasted_iota(jnp.int32, (8, TILE), 0)
        classes = jnp.concatenate(
            [cls_ref[pl.ds(2 * i, 1), :], cls_ref[pl.ds(2 * i + 1, 1), :]], axis=1
        )
        hot = jnp.where(row8 == classes, 1.0, 0.0).astype(F32)
        docs = jnp.where(row8 == 0, doc_tile(i), 0.0)
        onehot[i] = jnp.concatenate([hot, hot, hot, docs], axis=0).astype(BF16)
        wide = lax.dot_general(
            onehot[i], table[:, : 10 * HALF], DIM0, preferred_element_type=F32
        )
        t_pos = lax.broadcasted_iota(jnp.int32, (HALF, HALF), 0)
        s_pos = lax.broadcasted_iota(jnp.int32, (HALF, HALF), 1)
        apart = t_pos ^ s_pos
        causal = s_pos <= t_pos
        for a in range(2):
            rows = slice(a * HALF, (a + 1) * HALF)
            doc_t = wide[rows, 9 * HALF : 10 * HALF]
            weight = wide[rows, :HALF]
            for level in range(1, 8):
                column = wide[rows, level * HALF : (level + 1) * HALF]
                weight = jnp.where(apart >= 1 << (level - 1), column, weight)
            allowed = causal & (doc_t == doc_row(2 * i + a))
            grid[i, rows, rows] = jnp.where(allowed, weight, 0.0)
            if a == 1:
                weight = wide[rows, 8 * HALF : 9 * HALF]
                grid[i, rows, :HALF] = jnp.where(doc_t == doc_row(2 * i), weight, 0.0)
            else:
                grid[i, rows, HALF:] = jnp.zeros((HALF, HALF), F32)

    ylow[...] = jnp.zeros_like(ylow)
    ymask[...] = jnp.zeros_like(ymask)
    load_v.wait()

    for d in (1, 7, 2, 6, 3, 5, 4):
        k_copies[d].wait_recv()
        k_partner(d).start()
    for d in (0, 1, 7, 2, 6, 3, 5, 4):
        k_partner(d).wait_recv()

    def unpacked(gathered, j):
        wide = gathered[:, :, :, pl.ds(pl.multiple_of(j * TILE, TILE), TILE)].astype(F32)
        return [wide[:, :, 8 * a : 8 * a + 8, :].reshape(HALF, TILE) for a in range(2)]

    @pl.loop(0, NT // 2)
    def _(j):
        for a, keys in enumerate(unpacked(kg, j)):
            i = a * (NT // 2) + j
            docs = doc_tile(i)
            kept = jnp.where(docs == docs[:, TILE - 1 : TILE], keys, 0.0)
            kt[i] = keys.astype(BF16)
            part = dot(kept.astype(BF16), v[pl.ds(pl.multiple_of(i * TILE, TILE), TILE), :])
            state[i] = part
            left9[i] = part.astype(BF16)

    level_states = [state[i] for i in range(NT)]
    pairs = [
        level_states[2 * j + 1] + same(last_doc(2 * j), last_doc(2 * j + 1)) * level_states[2 * j]
        for j in range(4)
    ]
    for j in range(4):
        left10[j] = pairs[j].astype(BF16)
    quads = [
        pairs[2 * j + 1] + same(last_doc(4 * j + 1), last_doc(4 * j + 3)) * pairs[2 * j]
        for j in range(2)
    ]
    left11[...] = quads[0].astype(BF16)
    tail = quads[1] + same(last_doc(3), last_doc(7)) * quads[0]
    tag = jnp.broadcast_to(last_doc(7), (16, WIDTH)).astype(BF16)
    for p in range(X):
        tails[p, :QROWS] = tail[p * QROWS : (p + 1) * QROWS].astype(BF16)
        tails[p, QROWS:] = tag

    x_copies = {}
    for d in (2, 1, 3):
        x_copies[d] = remote(
            tails.at[(x + d) % X], xbuf.at[x], xs_sem.at[d], xr_sem.at[d], at_x(d)
        )
        x_copies[d].start()
    xbuf[x] = tails[x]

    for d in Z_ORDER:
        q_copies[d].wait_recv()
    q_partner = remote(qg.at[c], qg.at[c], qps_sem.at[0], qpr_sem.at[0], partner)
    q_partner.start()

    for d in (1, 3, 2):
        x_copies[d].wait_recv()
    ends = [xbuf[p, QROWS:].astype(F32)[0:1, 0:1] for p in range(X)]
    terms = [xbuf[p, :QROWS].astype(F32) for p in range(X)]
    low_pair = terms[1] + same(ends[0], ends[1]) * terms[0]
    high_pair = terms[3] + same(ends[2], ends[3]) * terms[2]
    row_tail = high_pair + same(ends[1], ends[3]) * low_pair
    ysend[:QROWS] = row_tail.astype(BF16)
    ysend[QROWS:] = jnp.broadcast_to(ends[3], (16, WIDTH)).astype(BF16)

    def y_copy(d):
        return remote(ysend, ybuf.at[y], ys_sem.at[d], yr_sem.at[d], at_y((y + d) % Y))

    for d in (4, 3, 5, 2, 6, 1, 7):

        @pl.when(y + d < Y)
        def _():
            y_copy(d).start()

    blank = jnp.zeros((QROWS, WIDTH), BF16)
    xlow[0, :QROWS] = blank
    xlow[0, QROWS:] = blank
    xlow[1, :QROWS] = xbuf[0, :QROWS]
    xlow[1, QROWS:] = blank
    xlow[2, :QROWS] = blank
    xlow[2, QROWS:] = low_pair.astype(BF16)
    xlow[3, :QROWS] = xbuf[2, :QROWS]
    xlow[3, QROWS:] = low_pair.astype(BF16)
    a_copies = {}
    for d in (2, 1, 3):
        a_copies[d] = remote(
            xlow.at[(x + d) % X], xout.at[x], as_sem.at[d], ar_sem.at[d], at_x(d)
        )
        a_copies[d].start()
    xout[x] = xlow[x]

    q_partner.wait_recv()

    def near_tile(i, queries):
        turned = queries.T
        rows = pl.ds(pl.multiple_of(i * TILE, TILE), TILE)
        scores = dot(turned.astype(BF16), kt[i])
        weighted = (scores * grid[i]).astype(BF16)
        total = dot(weighted, v[rows, :])
        wide = lax.dot_general(
            onehot[i], table[:, 9 * HALF :], DIM0, preferred_element_type=F32
        )
        doc_t = wide[:, :HALF]
        mids = []
        for b in range(MID_LEVELS):
            end = jnp.maximum((i >> b << b) - 1, 0)
            end_doc = doc_row(2 * end + 1)[:, HALF - 1 : HALF]
            present = jnp.where((i >> b) % 2 == 1, 1.0, 0.0).astype(F32)
            weight = jnp.where(doc_t == end_doc, wide[:, (1 + b) * HALF : (2 + b) * HALF], 0.0)
            mids.append((weight * (turned * present)).astype(BF16))
        lefts = [
            left9[jnp.maximum(i - 1, 0)],
            left10[jnp.maximum((i >> 1) - 1, 0)],
            left11[...],
        ]
        total = total + dot(jnp.concatenate(mids, axis=1), jnp.concatenate(lefts, axis=0))
        near[i] = total
        kept = jnp.where(doc_t == first_doc, turned, 0.0)
        for b in range(FAR_LEVELS):
            start = (1 + MID_LEVELS + b) * HALF
            qw[i, :, b * HALF : (b + 1) * HALF] = (wide[:, start : start + HALF] * kept).astype(BF16)

    @pl.loop(0, NT // 2)
    def _(j):
        for a, queries in enumerate(unpacked(qg, j)):
            near_tile(a * (NT // 2) + j, queries)

    for d in range(1, Y):

        @pl.when(y >= d)
        def _():
            y_copy(d).wait_recv()

    def y_row(row):
        return ybuf[row, :QROWS].astype(F32)

    def y_end(row):
        return ybuf[row, QROWS:].astype(F32)[0:1, 0:1]

    @pl.when(y % 2 == 1)
    def _():
        ylow[:QROWS] = ybuf[y - 1, :QROWS]
        ymask[0] = jnp.broadcast_to(same(y_end(y - 1), first_doc), (8, HALF))

    @pl.when((y // 2) % 2 == 1)
    def _():
        base = (y // 4) * 4
        merged = y_row(base + 1) + same(y_end(base), y_end(base + 1)) * y_row(base)
        ylow[QROWS : 2 * QROWS] = merged.astype(BF16)
        ymask[1] = jnp.broadcast_to(same(y_end(base + 1), first_doc), (8, HALF))

    @pl.when(y >= 4)
    def _():
        early = y_row(1) + same(y_end(0), y_end(1)) * y_row(0)
        late = y_row(3) + same(y_end(2), y_end(3)) * y_row(2)
        merged = late + same(y_end(1), y_end(3)) * early
        ylow[2 * QROWS :] = merged.astype(BF16)
        ymask[2] = jnp.broadcast_to(same(y_end(3), first_doc), (8, HALF))

    b_copies = {}
    for d in (2, 1, 3):
        b_copies[d] = remote(ylow, yout.at[x], bs_sem.at[d], br_sem.at[d], at_x(d))
        b_copies[d].start()
    yout[x] = ylow[...]

    for d in (1, 3, 2):
        a_copies[d].wait_recv()
    before = xbuf[jnp.maximum(x - 1, 0), QROWS:].astype(F32)[0:1, 0:1]
    x_masks = [same(before, first_doc), same(ends[1], first_doc)]
    for b in range(2):
        rows = xout[:, b * QROWS : (b + 1) * QROWS, :].astype(F32).reshape(HALF, WIDTH)
        bucket[b * HALF : (b + 1) * HALF] = (rows * x_masks[b]).astype(BF16)

    @pl.loop(0, NT)
    def _(i):
        near[i] = near[i] + dot(qw[i, :, : 2 * HALF], bucket[: 2 * HALF])

    for d in (1, 3, 2):
        b_copies[d].wait_recv()
    for b in range(3):
        rows = yout[:, b * QROWS : (b + 1) * QROWS, :].astype(F32).reshape(HALF, WIDTH)
        mask = ymask[b][0:1, 0:1]
        bucket[(2 + b) * HALF : (3 + b) * HALF] = (rows * mask).astype(BF16)

    @pl.loop(0, NT)
    def _(i):
        total = near[i] + dot(qw[i, :, 2 * HALF :], bucket[2 * HALF :])
        out_ref[pl.ds(pl.multiple_of(i * TILE, TILE), TILE), :] = total.astype(BF16)

    for d in range(1, Z):
        k_copies[d].wait_send()
        q_copies[d].wait_send()
    for d in range(Z):
        k_partner(d).wait_send()
    q_partner.wait_send()
    for d in range(1, X):
        x_copies[d].wait_send()
        a_copies[d].wait_send()
        b_copies[d].wait_send()
    for d in range(1, Y):

        @pl.when(y + d < Y)
        def _():
            y_copy(d).wait_send()


def local(queries, key_vectors, values, level_table, level_class, doc_ids):
    tokens, width = values.shape
    vmem = pl.BlockSpec(memory_space=pltpu.VMEM)
    hbm = pl.BlockSpec(memory_space=pl.ANY)
    dma = pltpu.SemaphoreType.DMA
    return pl.pallas_call(
        body,
        out_shape=jax.ShapeDtypeStruct((tokens, width), BF16),
        in_specs=[hbm, hbm, hbm, vmem, vmem, vmem],
        out_specs=vmem,
        scratch_shapes=[
            pltpu.VMEM((8, tokens), BF16),
            pltpu.VMEM((8, tokens), BF16),
            pltpu.VMEM((tokens, width), BF16),
            pltpu.VMEM((2, Z, 16, tokens // 2), BF16),
            pltpu.VMEM((2, Z, 16, tokens // 2), BF16),
            pltpu.VMEM((NT, 32, TILE), BF16),
            pltpu.VMEM((32, 18 * HALF), BF16),
            pltpu.VMEM((NT, TILE, TILE), F32),
            pltpu.VMEM((NT, HALF, TILE), BF16),
            pltpu.VMEM((NT, HALF, WIDTH), F32),
            pltpu.VMEM((NT, HALF, WIDTH), BF16),
            pltpu.VMEM((4, HALF, WIDTH), BF16),
            pltpu.VMEM((HALF, WIDTH), BF16),
            pltpu.VMEM((X, TAGGED, WIDTH), BF16),
            pltpu.VMEM((X, TAGGED, WIDTH), BF16),
            pltpu.VMEM((X, 2 * QROWS, WIDTH), BF16),
            pltpu.VMEM((X, 2 * QROWS, WIDTH), BF16),
            pltpu.VMEM((TAGGED, WIDTH), BF16),
            pltpu.VMEM((Y, TAGGED, WIDTH), BF16),
            pltpu.VMEM((3 * QROWS, WIDTH), BF16),
            pltpu.VMEM((X, 3 * QROWS, WIDTH), BF16),
            pltpu.VMEM((3, 8, HALF), F32),
            pltpu.VMEM((FAR_LEVELS * HALF, WIDTH), BF16),
            pltpu.VMEM((NT, TILE, FAR_LEVELS * HALF), BF16),
            pltpu.VMEM((NT, TILE, WIDTH), F32),
            dma((3,)),
            dma((Z,)),
            dma((Z,)),
            dma((Z,)),
            dma((Z,)),
            dma((Z,)),
            dma((Z,)),
            dma((1,)),
            dma((1,)),
            dma((X,)),
            dma((X,)),
            dma((X,)),
            dma((X,)),
            dma((Y,)),
            dma((Y,)),
            dma((X,)),
            dma((X,)),
        ],
        compiler_params=pltpu.CompilerParams(
            collective_id=0, has_side_effects=True, vmem_limit_bytes=40 * 1024 * 1024
        ),
        name="block_and_levels",
    )(
        key_vectors.T,
        queries.T,
        values,
        level_table,
        level_class.reshape(tokens // HALF, HALF),
        doc_ids.reshape(tokens // HALF, HALF),
    )


def solution(mesh):
    in_specs = (P("seq", "head"), P("seq", "head"), P("seq", "head"), P(), P("seq"), P("seq"))
    out_specs = P("seq", "head")
    return jax.shard_map(local, mesh=mesh, in_specs=in_specs, out_specs=out_specs, check_vma=False)
```

profile of v0, /device:TPU:1, one launch (start us, length us, event | category | flops | bytes accessed | tf_op | source)
XLA Modules:
  0.0 47.8 jit_solution(5069530715070226044)
XLA Ops:
  0.0 0.0 copy-start.5
  0.0 0.7 %copy-done.5 = f32[8,17]{1,0:T(8,128)S(1)} copy-done((f32[8,17]{1,0:T(8,128)S(1)}, f32[8,17]{1,0:T(8,128)}, u32[]{:S(2)}) %copy-start.5) | copy-done | bytes 568
  0.7 0.0 copy-start
  0.7 1.2 %copy-done = bf16[2048,256]{1,0:T(8,128)(2,1)S(1)} copy-done((bf16[2048,256]{1,0:T(8,128)(2,1)S(1)}, bf16[2048,256]{1,0:T(8,128)(2,1)}, u32[]{:S(2)}) %copy-start) | copy-done | bytes 1048600
  1.9 0.0 copy-start.1
  1.9 0.8 %copy-done.1 = bf16[2048,8]{0,1:T(8,128)(2,1)S(1)} copy-done((bf16[2048,8]{0,1:T(8,128)(2,1)S(1)}, bf16[2048,8]{0,1:T(8,128)(2,1)}, u32[]{:S(2)}) %copy-start.1) | copy-done | bytes 32792
  2.7 0.0 copy-start.2
  2.7 0.8 %copy-done.2 = bf16[2048,8]{0,1:T(8,128)(2,1)S(1)} copy-done((bf16[2048,8]{0,1:T(8,128)(2,1)S(1)}, bf16[2048,8]{0,1:T(8,128)(2,1)}, u32[]{:S(2)}) %copy-start.2) | copy-done | bytes 32792
  3.4 0.0 copy-start.3
  3.4 0.7 %copy-done.3 = s32[2048]{0:T(1024)S(1)} copy-done((s32[2048]{0:T(1024)S(1)}, s32[2048]{0:T(1024)}, u32[]{:S(2)}) %copy-start.3) | copy-done | bytes 8216
  4.1 0.0 copy-start.4
  4.1 0.7 %copy-done.4 = s32[2048]{0:T(1024)S(1)} copy-done((s32[2048]{0:T(1024)S(1)}, s32[2048]{0:T(1024)}, u32[]{:S(2)}) %copy-start.4) | copy-done | bytes 8216
  4.8 41.9 %block_and_levels.1 = bf16[2048,256]{1,0:T(8,128)(2,1)S(1)} custom-call(bf16[8,2048]{1,0:T(8,128)(2,1)S(1)} %bitcast.4, bf16[8,2048]{1,0:T(8,128)(2,1)S(1)} %bitcast.5, bf16[2048,256]{1,0:T(8,128)(2,1)S(1)} %copy-done, f32[8,17]{1,0:T(8,128)S(1)} %copy-done.5, s32[16,128]{1,0:T(8,128)S(1)} %bitcast.6, s32[16,128]{1,0:T(8,128)S(1)} %bitcast.7), custom_call_target="tpu_custom_call" | custom-call | tf_op jit(solution)/shard_map/block_and_levels/pallas_call | solution.py:420
  46.8 1.0 %copy.8 = bf16[2048,256]{1,0:T(8,128)(2,1)} copy(bf16[2048,256]{1,0:T(8,128)(2,1)S(1)} %block_and_levels.1) | data formatting | bytes 2097152
Async XLA Ops:
  0.0 0.7 %copy-start.5 = (f32[8,17]{1,0:T(8,128)S(1)}, f32[8,17]{1,0:T(8,128)}, u32[]{:S(2)}) copy-start(f32[8,17]{1,0:T(8,128)} %tab_ref.1) | copy-start | bytes 1636
  0.7 1.2 %copy-start = (bf16[2048,256]{1,0:T(8,128)(2,1)S(1)}, bf16[2048,256]{1,0:T(8,128)(2,1)}, u32[]{:S(2)}) copy-start(bf16[2048,256]{1,0:T(8,128)(2,1)} %v_hbm.1) | copy-start | bytes 3145732
  1.9 0.8 %copy-start.1 = (bf16[2048,8]{0,1:T(8,128)(2,1)S(1)}, bf16[2048,8]{0,1:T(8,128)(2,1)}, u32[]{:S(2)}) copy-start(bf16[2048,8]{0,1:T(8,128)(2,1)} %param.7) | copy-start | bytes 98308
  2.7 0.8 %copy-start.2 = (bf16[2048,8]{0,1:T(8,128)(2,1)S(1)}, bf16[2048,8]{0,1:T(8,128)(2,1)}, u32[]{:S(2)}) copy-start(bf16[2048,8]{0,1:T(8,128)(2,1)} %param.6) | copy-start | bytes 98308
  3.4 0.7 %copy-start.3 = (s32[2048]{0:T(1024)S(1)}, s32[2048]{0:T(1024)}, u32[]{:S(2)}) copy-start(s32[2048]{0:T(1024)} %param.10) | copy-start | bytes 24580
  4.1 0.7 %copy-start.4 = (s32[2048]{0:T(1024)S(1)}, s32[2048]{0:T(1024)}, u32[]{:S(2)}) copy-start(s32[2048]{0:T(1024)} %param.11) | copy-start | bytes 24580
where the time goes:
time: 48.2 us; the launch traced here: 47.8 us
  Pallas kernels  41.9 us (87%)
  local copies, waits for them, and re-layouts  5.79 us (12%)
    pallas_call x1, Pallas kernels, local(): pl.pallas_call(body, out_shape=jax.ShapeDtypeStruct((tokens, width), BF16...  41.9 us
    unnamed x13, local copies, waits for them, and re-layouts  5.79 us

commit v1 on v0

v1 whole, which is shorter than its diff:
```python
import jax
import jax.numpy as jnp
from jax import lax
from jax.experimental import pallas as pl
from jax.experimental.pallas import tpu as pltpu
from jax.sharding import PartitionSpec as P

MESH = pl.DeviceIdType.MESH
F32 = jnp.float32
BF16 = jnp.bfloat16

X = 4
Y = 8
Z = 8
TILE = 256
NT = 8
HALF = 128
WIDTH = 256
NEAR_LEVELS = 9
MID_LEVELS = 3
X_LEVELS = 2
Y_LEVELS = 3
FAR_LEVELS = X_LEVELS + Y_LEVELS
QROWS = 32
TAG = 16
TWO_HOPS = (2, 6, 1, 7)
FARTHEST_FIRST = (4, 3, 5, 2, 6, 1, 7)
DIM0 = (((0,), (0,)), ((), ()))


def dot(a, b):
    return jnp.dot(a, b, preferred_element_type=F32)


def same(a, b):
    return jnp.where(a == b, 1.0, 0.0).astype(F32)


def body(
    k_hbm,
    q_hbm,
    v_hbm,
    tab_hbm,
    cls_hbm,
    doc_hbm,
    near,
    qy,
    by,
    tab_ref,
    cls_ref,
    doc_ref,
    k8,
    q8,
    v,
    kg,
    qg,
    onehot,
    table,
    grid,
    kt,
    state,
    left9,
    left10,
    left11,
    tails,
    xtag,
    ytag,
    xbuf,
    xlow,
    xout,
    ysend,
    ybuf,
    ylow,
    yout,
    bx,
    qx,
    in_sem,
    ks_sem,
    kr_sem,
    kps_sem,
    kpr_sem,
    qs_sem,
    qr_sem,
    qps_sem,
    qpr_sem,
    xs_sem,
    xr_sem,
    as_sem,
    ar_sem,
    ys_sem,
    yr_sem,
    bs_sem,
    br_sem,
    ts_sem,
    tr_sem,
    us_sem,
    ur_sem,
    ready_sem,
):
    seq = lax.axis_index("seq")
    head = lax.axis_index("head")
    x = lax.rem(seq, X)
    y = lax.div(seq, X)
    z = lax.div(head, 2)
    c = lax.rem(head, 2)

    def at_z(d):
        return {"seq": seq, "head": lax.rem(z + d, Z) * 2 + c}

    def at_x(d):
        return {"seq": y * X + lax.rem(x + d, X), "head": head}

    def at_y(row):
        return {"seq": row * X + x, "head": head}

    partner = {"seq": seq, "head": z * 2 + (1 - c)}

    def remote(src, dst, send, recv, device):
        return pltpu.make_async_remote_copy(
            src_ref=src,
            dst_ref=dst,
            send_sem=send,
            recv_sem=recv,
            device_id=device,
            device_id_type=MESH,
        )

    load_k = pltpu.make_async_copy(k_hbm, k8, in_sem.at[0])
    load_q = pltpu.make_async_copy(q_hbm, q8, in_sem.at[1])
    load_v = pltpu.make_async_copy(v_hbm, v, in_sem.at[2])
    load_k.start()
    load_q.start()
    small_loads = [
        pltpu.make_async_copy(tab_hbm, tab_ref, in_sem.at[3]),
        pltpu.make_async_copy(cls_hbm, cls_ref, in_sem.at[4]),
        pltpu.make_async_copy(doc_hbm, doc_ref, in_sem.at[5]),
    ]
    for load in small_loads:
        load.start()
    load_v.start()

    barrier = pltpu.get_barrier_semaphore()
    peers = [at_z(d) for d in TWO_HOPS] + [at_x(d) for d in (2, 1, 3)]
    peers = peers + [at_y(lax.rem(y + d, Y)) for d in TWO_HOPS] + [partner]
    for peer in peers:
        pl.semaphore_signal(barrier, inc=1, device_id=peer, device_id_type=MESH)

    def pack(shard):
        wide = shard[...].astype(F32)
        return jnp.concatenate([wide[:, :1024], wide[:, 1024:]], axis=0).astype(BF16)

    load_k.wait()
    kg[c, z] = pack(k8)
    pl.semaphore_wait(barrier, len(peers))

    def gather(slots, send, recv):
        def own(d):
            return remote(slots.at[c, z], slots.at[c, z], send.at[d], recv.at[d], at_z(d))

        def onward(back, hop, index, part):
            slot = slots.at[c, lax.rem(z + Z - back, Z), :, part]
            return remote(slot, slot, send.at[index], recv.at[index], at_z(hop))

        steps = {d: own(d) for d in TWO_HOPS}
        steps[3] = onward(2, 1, 3, pl.ds(0, 1024))
        steps[5] = onward(6, 7, 5, pl.ds(0, 1024))
        steps[4] = onward(2, 2, 4, pl.ds(0, 512))
        steps[8] = onward(6, 6, 8, pl.ds(512, 512))
        return steps

    k_steps = gather(kg, ks_sem, kr_sem)
    q_steps = gather(qg, qs_sem, qr_sem)
    for d in TWO_HOPS:
        k_steps[d].start()

    def k_partner(d):
        slot = kg.at[c, lax.rem(z + Z - d, Z)]
        return remote(slot, slot, kps_sem.at[d], kpr_sem.at[d], partner)

    k_partner(0).start()
    for d in (2, 6):
        row = lax.rem(y + d, Y)
        pl.semaphore_signal(
            ready_sem.at[d // 4], inc=1, device_id=at_y(row), device_id_type=MESH
        )
    for load in small_loads:
        load.wait()
    load_q.wait()
    qg[c, z] = pack(q8)

    def last_doc(i):
        return doc_ref[2 * i + 1 : 2 * i + 2, HALF - 1 : HALF].astype(F32)

    xtag[x] = jnp.broadcast_to(last_doc(NT - 1), (TAG, HALF)).astype(BF16)
    t_copies = {}
    for d in (2, 1, 3):
        t_copies[d] = remote(xtag.at[x], xtag.at[x], ts_sem.at[d], tr_sem.at[d], at_x(d))
        t_copies[d].start()

    for order, level in enumerate(list(range(NEAR_LEVELS)) + [None] + list(range(NEAR_LEVELS, 17))):
        columns = slice(order * HALF, (order + 1) * HALF)
        if level is None:
            row = lax.broadcasted_iota(jnp.int32, (32, HALF), 0)
            table[:, columns] = jnp.where(row == 24, 1.0, 0.0).astype(BF16)
        else:
            weight = jnp.broadcast_to(tab_ref[:, level : level + 1], (8, HALF))
            high = weight.astype(BF16).astype(F32)
            middle = (weight - high).astype(BF16).astype(F32)
            low = weight - high - middle
            parts = [high, middle, low, jnp.zeros_like(low)]
            table[:, columns] = jnp.concatenate(parts, axis=0).astype(BF16)

    def doc_row(block):
        return doc_ref[pl.ds(block, 1), :].astype(F32)

    def doc_tile(i):
        return jnp.concatenate([doc_row(2 * i), doc_row(2 * i + 1)], axis=1)

    first_doc = doc_ref[0:1, 0:1].astype(F32)

    def grid_tile(i):
        row8 = lax.broadcasted_iota(jnp.int32, (8, TILE), 0)
        classes = jnp.concatenate(
            [cls_ref[pl.ds(2 * i, 1), :], cls_ref[pl.ds(2 * i + 1, 1), :]], axis=1
        )
        hot = jnp.where(row8 == classes, 1.0, 0.0).astype(F32)
        docs = jnp.where(row8 == 0, doc_tile(i), 0.0)
        onehot[i] = jnp.concatenate([hot, hot, hot, docs], axis=0).astype(BF16)
        wide = lax.dot_general(
            onehot[i], table[:, : 10 * HALF], DIM0, preferred_element_type=F32
        )
        t_pos = lax.broadcasted_iota(jnp.int32, (HALF, HALF), 0)
        s_pos = lax.broadcasted_iota(jnp.int32, (HALF, HALF), 1)
        apart = t_pos ^ s_pos
        causal = s_pos <= t_pos
        for a in range(2):
            rows = slice(a * HALF, (a + 1) * HALF)
            doc_t = wide[rows, 9 * HALF : 10 * HALF]
            weight = wide[rows, :HALF]
            for level in range(1, 8):
                column = wide[rows, level * HALF : (level + 1) * HALF]
                weight = jnp.where(apart >= 1 << (level - 1), column, weight)
            allowed = causal & (doc_t == doc_row(2 * i + a))
            grid[i, rows, rows] = jnp.where(allowed, weight, 0.0)
            if a == 1:
                weight = wide[rows, 8 * HALF : 9 * HALF]
                grid[i, rows, :HALF] = jnp.where(doc_t == doc_row(2 * i), weight, 0.0)
            else:
                grid[i, rows, HALF:] = jnp.zeros((HALF, HALF), F32)

    @pl.loop(0, NT // 2)
    def _(i):
        grid_tile(i)

    for d, first, second in ((2, 3, 4), (6, 5, 8)):
        k_steps[d].wait_recv()
        k_steps[first].start()
        k_steps[second].start()
    k_partner(2).start()
    k_partner(6).start()
    for d in (1, 7):
        k_steps[d].wait_recv()
        k_partner(d).start()

    for d in (1, 3, 2):
        t_copies[d].wait_recv()
    ytag[y] = xtag[X - 1]
    for side in range(2):
        pl.semaphore_wait(ready_sem.at[side], 1)

    def u_copy(d):
        row = lax.rem(y + d, Y)
        return remote(ytag.at[y], ytag.at[y], us_sem.at[d], ur_sem.at[d], at_y(row))

    for d in FARTHEST_FIRST:

        @pl.when(y + d < Y)
        def _():
            u_copy(d).start()

    @pl.loop(NT // 2, NT)
    def _(i):
        grid_tile(i)

    by[...] = jnp.zeros_like(by)
    load_v.wait()
    for d in (3, 5):
        k_steps[d].wait_recv()
        k_partner(d).start()
    k_steps[4].wait_recv()
    k_steps[8].wait_recv()
    k_partner(4).start()
    for d in TWO_HOPS:
        q_steps[d].start()
    for d in (0, 2, 6, 1, 7, 3, 5, 4):
        k_partner(d).wait_recv()

    def unpacked(gathered, j):
        wide = gathered[:, :, :, pl.ds(pl.multiple_of(j * TILE, TILE), TILE)].astype(F32)
        return [wide[:, :, 8 * a : 8 * a + 8, :].reshape(HALF, TILE) for a in range(2)]

    @pl.loop(0, NT // 2)
    def _(j):
        for a, keys in enumerate(unpacked(kg, j)):
            i = a * (NT // 2) + j
            docs = doc_tile(i)
            kept = jnp.where(docs == docs[:, TILE - 1 : TILE], keys, 0.0)
            kt[i] = keys.astype(BF16)
            part = dot(kept.astype(BF16), v[pl.ds(pl.multiple_of(i * TILE, TILE), TILE), :])
            state[i] = part
            left9[i] = part.astype(BF16)

    level_states = [state[i] for i in range(NT)]
    pairs = [
        level_states[2 * j + 1] + same(last_doc(2 * j), last_doc(2 * j + 1)) * level_states[2 * j]
        for j in range(4)
    ]
    for j in range(4):
        left10[j] = pairs[j].astype(BF16)
    quads = [
        pairs[2 * j + 1] + same(last_doc(4 * j + 1), last_doc(4 * j + 3)) * pairs[2 * j]
        for j in range(2)
    ]
    left11[...] = quads[0].astype(BF16)
    tail = quads[1] + same(last_doc(3), last_doc(7)) * quads[0]
    for p in range(X):
        tails[p] = tail[p * QROWS : (p + 1) * QROWS].astype(BF16)

    x_copies = {}
    for d in (2, 1, 3):
        x_copies[d] = remote(
            tails.at[lax.rem(x + d, X)], xbuf.at[x], xs_sem.at[d], xr_sem.at[d], at_x(d)
        )
        x_copies[d].start()
    xbuf[x] = tails[x]

    for d, first, second in ((2, 3, 4), (6, 5, 8)):
        q_steps[d].wait_recv()
        q_steps[first].start()
        q_steps[second].start()

    for d in (1, 3, 2):
        x_copies[d].wait_recv()
    ends = [xtag[p].astype(F32)[0:1, 0:1] for p in range(X)]
    terms = [xbuf[p].astype(F32) for p in range(X)]
    low_pair = terms[1] + same(ends[0], ends[1]) * terms[0]
    high_pair = terms[3] + same(ends[2], ends[3]) * terms[2]
    row_tail = high_pair + same(ends[1], ends[3]) * low_pair
    ysend[...] = row_tail.astype(BF16)

    def y_copy(d):
        row = lax.rem(y + d, Y)
        return remote(ysend, ybuf.at[y], ys_sem.at[d], yr_sem.at[d], at_y(row))

    for d in FARTHEST_FIRST:

        @pl.when(y + d < Y)
        def _():
            y_copy(d).start()

    blank = jnp.zeros((QROWS, WIDTH), BF16)
    xlow[0, :QROWS] = blank
    xlow[0, QROWS:] = blank
    xlow[1, :QROWS] = xbuf[0]
    xlow[1, QROWS:] = blank
    xlow[2, :QROWS] = blank
    xlow[2, QROWS:] = low_pair.astype(BF16)
    xlow[3, :QROWS] = xbuf[2]
    xlow[3, QROWS:] = low_pair.astype(BF16)
    a_copies = {}
    for d in (2, 1, 3):
        a_copies[d] = remote(
            xlow.at[lax.rem(x + d, X)], xout.at[x], as_sem.at[d], ar_sem.at[d], at_x(d)
        )
        a_copies[d].start()
    xout[x] = xlow[x]

    for d in (1, 7, 3, 5, 4, 8):
        q_steps[d].wait_recv()
    q_partner = remote(qg.at[c], qg.at[c], qps_sem.at[0], qpr_sem.at[0], partner)
    q_partner.start()
    q_partner.wait_recv()

    def near_tile(i, queries):
        turned = queries.T
        rows = pl.ds(pl.multiple_of(i * TILE, TILE), TILE)
        scores = dot(turned.astype(BF16), kt[i])
        weighted = (scores * grid[i]).astype(BF16)
        total = dot(weighted, v[rows, :])
        wide = lax.dot_general(
            onehot[i], table[:, 9 * HALF :], DIM0, preferred_element_type=F32
        )
        doc_t = wide[:, :HALF]
        mids = []
        for b in range(MID_LEVELS):
            end = jnp.maximum((i >> b << b) - 1, 0)
            end_doc = doc_row(2 * end + 1)[:, HALF - 1 : HALF]
            present = jnp.where((i >> b) % 2 == 1, 1.0, 0.0).astype(F32)
            weight = jnp.where(doc_t == end_doc, wide[:, (1 + b) * HALF : (2 + b) * HALF], 0.0)
            mids.append((weight * (turned * present)).astype(BF16))
        lefts = [
            left9[jnp.maximum(i - 1, 0)],
            left10[jnp.maximum((i >> 1) - 1, 0)],
            left11[...],
        ]
        total = total + dot(jnp.concatenate(mids, axis=1), jnp.concatenate(lefts, axis=0))
        near[i] = total
        kept = jnp.where(doc_t == first_doc, turned, 0.0)
        for b in range(FAR_LEVELS):
            start = (1 + MID_LEVELS + b) * HALF
            target, place = (qx, b) if b < X_LEVELS else (qy, b - X_LEVELS)
            columns = slice(place * HALF, (place + 1) * HALF)
            target[i, :, columns] = (wide[:, start : start + HALF] * kept).astype(BF16)

    @pl.loop(0, NT // 4)
    def _(j):
        for a, queries in enumerate(unpacked(qg, j)):
            near_tile(a * (NT // 2) + j, queries)

    for d in range(1, Y):

        @pl.when(y >= d)
        def _():
            u_copy(d).wait_recv()

    def y_row(row):
        return ybuf[row].astype(F32)

    def y_end(row):
        return ytag[row].astype(F32)[0:1, 0:1]

    def b_copy(b, d):
        index = b * X + d
        return remote(ylow.at[b], yout.at[x, b], bs_sem.at[index], br_sem.at[index], at_x(d))

    def hand_on(b, merged):
        ylow[b] = merged
        yout[x, b] = merged
        for d in (2, 1, 3):
            b_copy(b, d).start()

    bits = [lax.rem(y, 2) == 1, lax.rem(lax.div(y, 2), 2) == 1, y >= 4]
    four = lax.div(y, 4) * 4

    @pl.when(bits[0])
    def _():
        y_copy(1).wait_recv()
        hand_on(0, ybuf[y - 1])

    @pl.when(bits[1])
    def _():
        for d in range(2):
            y_copy(y - four - d).wait_recv()
        merged = y_row(four + 1) + same(y_end(four), y_end(four + 1)) * y_row(four)
        hand_on(1, merged.astype(BF16))

    @pl.when(bits[2])
    def _():
        for d in range(4):
            y_copy(y - d).wait_recv()
        early = y_row(1) + same(y_end(0), y_end(1)) * y_row(0)
        late = y_row(3) + same(y_end(2), y_end(3)) * y_row(2)
        merged = late + same(y_end(1), y_end(3)) * early
        hand_on(2, merged.astype(BF16))

    @pl.loop(NT // 4, NT // 2)
    def _(j):
        for a, queries in enumerate(unpacked(qg, j)):
            near_tile(a * (NT // 2) + j, queries)

    for d in (1, 3, 2):
        a_copies[d].wait_recv()
    before = xtag[jnp.maximum(x - 1, 0)].astype(F32)[0:1, 0:1]
    x_masks = [same(before, first_doc), same(ends[1], first_doc)]
    for b in range(2):
        rows = xout[:, b * QROWS : (b + 1) * QROWS, :].astype(F32).reshape(HALF, WIDTH)
        bx[b * HALF : (b + 1) * HALF] = (rows * x_masks[b]).astype(BF16)

    @pl.loop(0, NT // 2)
    def _(j):
        for i in (2 * j, 2 * j + 1):
            near[i] = near[i] + dot(qx[i], bx[...])

    y_ends = [y - 1, four + 1, 3]
    for b in range(Y_LEVELS):

        @pl.when(bits[b])
        def _():
            for d in (1, 3, 2):
                b_copy(b, d).wait_recv()
            rows = yout[:, b].astype(F32).reshape(HALF, WIDTH)
            mask = same(y_end(y_ends[b]), first_doc)
            by[b * HALF : (b + 1) * HALF] = (rows * mask).astype(BF16)

    for step in k_steps:
        k_steps[step].wait_send()
        q_steps[step].wait_send()
    for d in range(Z):
        k_partner(d).wait_send()
    q_partner.wait_send()
    for d in range(1, X):
        t_copies[d].wait_send()
        x_copies[d].wait_send()
        a_copies[d].wait_send()
    for b in range(Y_LEVELS):

        @pl.when(bits[b])
        def _():
            for d in range(1, X):
                b_copy(b, d).wait_send()

    for d in range(1, Y):

        @pl.when(y + d < Y)
        def _():
            u_copy(d).wait_send()
            y_copy(d).wait_send()


def last(near, qy, by, out_hbm, out, out_sem):
    copies = []
    for i in range(NT):
        rows = pl.ds(i * TILE, TILE)
        out[rows, :] = (near[i] + dot(qy[i], by[...])).astype(BF16)
        copies.append(pltpu.make_async_copy(out.at[rows], out_hbm.at[rows], out_sem.at[i]))
        copies[i].start()
    for copy in copies:
        copy.wait()


def local(queries, key_vectors, values, level_table, level_class, doc_ids):
    tokens, width = values.shape
    vmem = pl.BlockSpec(memory_space=pltpu.VMEM)
    hbm = pl.BlockSpec(memory_space=pltpu.HBM)
    dma = pltpu.SemaphoreType.DMA
    arguments = (
        key_vectors.T,
        queries.T,
        values,
        level_table,
        level_class.reshape(tokens // HALF, HALF),
        doc_ids.reshape(tokens // HALF, HALF),
    )
    near, qy, by = pl.pallas_call(
        body,
        out_shape=[
            pltpu.VMEM((NT, TILE, WIDTH), F32),
            pltpu.VMEM((NT, TILE, Y_LEVELS * HALF), BF16),
            pltpu.VMEM((Y_LEVELS * HALF, WIDTH), BF16),
        ],
        in_specs=[hbm] * 6,
        out_specs=[vmem] * 3,
        scratch_shapes=[
            pltpu.VMEM(level_table.shape, F32),
            pltpu.VMEM((tokens // HALF, HALF), jnp.int32),
            pltpu.VMEM((tokens // HALF, HALF), jnp.int32),
            pltpu.VMEM((8, tokens), BF16),
            pltpu.VMEM((8, tokens), BF16),
            pltpu.VMEM((tokens, width), BF16),
            pltpu.VMEM((2, Z, 16, tokens // 2), BF16),
            pltpu.VMEM((2, Z, 16, tokens // 2), BF16),
            pltpu.VMEM((NT, 32, TILE), BF16),
            pltpu.VMEM((32, 18 * HALF), BF16),
            pltpu.VMEM((NT, TILE, TILE), F32),
            pltpu.VMEM((NT, HALF, TILE), BF16),
            pltpu.VMEM((NT, HALF, WIDTH), F32),
            pltpu.VMEM((NT, HALF, WIDTH), BF16),
            pltpu.VMEM((4, HALF, WIDTH), BF16),
            pltpu.VMEM((HALF, WIDTH), BF16),
            pltpu.VMEM((X, QROWS, WIDTH), BF16),
            pltpu.VMEM((X, TAG, HALF), BF16),
            pltpu.VMEM((Y, TAG, HALF), BF16),
            pltpu.VMEM((X, QROWS, WIDTH), BF16),
            pltpu.VMEM((X, 2 * QROWS, WIDTH), BF16),
            pltpu.VMEM((X, 2 * QROWS, WIDTH), BF16),
            pltpu.VMEM((QROWS, WIDTH), BF16),
            pltpu.VMEM((Y, QROWS, WIDTH), BF16),
            pltpu.VMEM((Y_LEVELS, QROWS, WIDTH), BF16),
            pltpu.VMEM((X, Y_LEVELS, QROWS, WIDTH), BF16),
            pltpu.VMEM((X_LEVELS * HALF, WIDTH), BF16),
            pltpu.VMEM((NT, TILE, X_LEVELS * HALF), BF16),
            dma((6,)),
            dma((Z + 1,)),
            dma((Z + 1,)),
            dma((Z,)),
            dma((Z,)),
            dma((Z + 1,)),
            dma((Z + 1,)),
            dma((1,)),
            dma((1,)),
            dma((X,)),
            dma((X,)),
            dma((X,)),
            dma((X,)),
            dma((Y,)),
            dma((Y,)),
            dma((Y_LEVELS * X,)),
            dma((Y_LEVELS * X,)),
            dma((X,)),
            dma((X,)),
            dma((Y,)),
            dma((Y,)),
            pltpu.SemaphoreType.REGULAR((2,)),
        ],
        compiler_params=pltpu.CompilerParams(
            collective_id=0, has_side_effects=True, vmem_limit_bytes=40 * 1024 * 1024
        ),
        name="blocks_and_states",
    )(*[pltpu.with_memory_space_constraint(a, pltpu.HBM) for a in arguments])
    return pl.pallas_call(
        last,
        out_shape=jax.ShapeDtypeStruct((tokens, width), BF16),
        in_specs=[vmem] * 3,
        out_specs=pl.BlockSpec(memory_space=pltpu.HBM),
        scratch_shapes=[pltpu.VMEM((tokens, width), BF16), dma((NT,))],
        compiler_params=pltpu.CompilerParams(vmem_limit_bytes=16 * 1024 * 1024),
        name="rows_before",
    )(near, qy, by)


def solution(mesh):
    in_specs = (P("seq", "head"), P("seq", "head"), P("seq", "head"), P(), P("seq"), P("seq"))
    out_specs = P("seq", "head")
    return jax.shard_map(local, mesh=mesh, in_specs=in_specs, out_specs=out_specs, check_vma=False)
```

time: 48.2 us -> 38.5 us (0.80)
  local copies, waits for them, and re-layouts: 5.79 us -> 0 us
  Pallas kernels: 41.9 us -> 38.3 us
    unnamed x13 -> x0, local copies, waits for them, and re-layouts: 5.79 us -> none
    pallas_call x1 -> x2, Pallas kernels: 41.9 us -> 38.3 us  [the longest x1 36.8 us: local(): pl.pallas_call(body, out_shape=[pltpu.VMEM((NT, TILE, WIDTH), F32), pltpu...]
where the time goes in v1:
time: 38.5 us; the launch traced here: 38.3 us
  Pallas kernels  38.3 us (99%)
    pallas_call x1, Pallas kernels, local(): pl.pallas_call(body, out_shape=[pltpu.VMEM((NT, TILE, WIDTH), F32), pltpu...  36.8 us
    pallas_call x1, Pallas kernels, local(): pl.pallas_call(last, out_shape=jax.ShapeDtypeStruct((tokens, width), BF16...  1.49 us

profile of v1, /device:TPU:1, one launch (start us, length us, event | category | flops | bytes accessed | tf_op | source)
XLA Modules:
  0.0 38.3 jit_solution(4434352179057280424)
XLA Ops:
  0.0 36.8 %blocks_and_states.1 = (f32[8,256,256]{2,1,0:T(8,128)S(1)}, bf16[8,256,384]{2,1,0:T(8,128)(2,1)S(1)}, bf16[384,256]{1,0:T(8,128)(2,1)S(1)}) custom-call(bf16[8,2048]{1,0:T(8,128)(2,1)} %bitcast.4, bf16[8,2048]{1,0:T(8,128)(2,1)} %bitcast.5, bf16[2048,256]{1,0:T(8,128)(2,1)} %v_hbm.1, f32[8,17]{1,0:T(8,128)} %tab_hbm.1, s32[16,128]{1,0:T(8,128)} %bitcast.6, ...), custom_call_target="tpu_custom_call" | custom-call | tf_op jit(solution)/shard_map/blocks_and_states/pallas_call | solution.py:544
  36.8 1.5 %rows_before.1 = bf16[2048,256]{1,0:T(8,128)(2,1)} custom-call(f32[8,256,256]{2,1,0:T(8,128)S(1)} %get-tuple-element.8.near, bf16[8,256,384]{2,1,0:T(8,128)(2,1)S(1)} %get-tuple-element.9.qy, bf16[384,256]{1,0:T(8,128)(2,1)S(1)} %get-tuple-element.10.by), custom_call_target="tpu_custom_call" | custom-call | tf_op jit(solution)/shard_map/rows_before/pallas_call | solution.py:610

commit v2 on v1

--- a/solution.py
+++ b/solution.py
@@ -21,7 +21,8 @@
 X_LEVELS = 2
 Y_LEVELS = 3
 FAR_LEVELS = X_LEVELS + Y_LEVELS
-QROWS = 32
+LANE = 64
+QROWS = 16
 TAG = 16
 TWO_HOPS = (2, 6, 1, 7)
 FARTHEST_FIRST = (4, 3, 5, 2, 6, 1, 7)
@@ -49,9 +50,8 @@
     tab_ref,
     cls_ref,
     doc_ref,
-    k8,
-    q8,
     v,
+    v_beside,
     kg,
     qg,
     onehot,
@@ -96,6 +96,8 @@
     us_sem,
     ur_sem,
     ready_sem,
+    vs_sem,
+    vr_sem,
 ):
     seq = lax.axis_index("seq")
     head = lax.axis_index("head")
@@ -109,6 +111,9 @@
 
     def at_x(d):
         return {"seq": y * X + lax.rem(x + d, X), "head": head}
+
+    def beside_x(d):
+        return {"seq": y * X + lax.rem(x + d, X), "head": z * 2 + (1 - c)}
 
     def at_y(row):
         return {"seq": row * X + x, "head": head}
@@ -125,8 +130,15 @@
             device_id_type=MESH,
         )
 
-    load_k = pltpu.make_async_copy(k_hbm, k8, in_sem.at[0])
-    load_q = pltpu.make_async_copy(q_hbm, q8, in_sem.at[1])
+    barrier = pltpu.get_barrier_semaphore()
+    peers = [at_z(d) for d in TWO_HOPS] + [at_x(d) for d in (2, 1, 3)]
+    peers = peers + [at_y(lax.rem(y + d, Y)) for d in TWO_HOPS]
+    peers = peers + [beside_x(d) for d in (2, 1, 3, 0)]
+    for peer in peers:
+        pl.semaphore_signal(barrier, inc=1, device_id=peer, device_id_type=MESH)
+
+    load_k = pltpu.make_async_copy(k_hbm, kg.at[c, z], in_sem.at[0])
+    load_q = pltpu.make_async_copy(q_hbm, qg.at[c, z], in_sem.at[1])
     load_v = pltpu.make_async_copy(v_hbm, v, in_sem.at[2])
     load_k.start()
     load_q.start()
@@ -139,23 +151,11 @@
         load.start()
     load_v.start()
 
-    barrier = pltpu.get_barrier_semaphore()
-    peers = [at_z(d) for d in TWO_HOPS] + [at_x(d) for d in (2, 1, 3)]
-    peers = peers + [at_y(lax.rem(y + d, Y)) for d in TWO_HOPS] + [partner]
-    for peer in peers:
-        pl.semaphore_signal(barrier, inc=1, device_id=peer, device_id_type=MESH)
-
-    def pack(shard):
-        wide = shard[...].astype(F32)
-        return jnp.concatenate([wide[:, :1024], wide[:, 1024:]], axis=0).astype(BF16)
-
-    load_k.wait()
-    kg[c, z] = pack(k8)
     pl.semaphore_wait(barrier, len(peers))
 
-    def gather(slots, send, recv):
+    def gather(shard, slots, send, recv):
         def own(d):
-            return remote(slots.at[c, z], slots.at[c, z], send.at[d], recv.at[d], at_z(d))
+            return remote(shard, slots.at[c, z], send.at[d], recv.at[d], at_z(d))
 
         def onward(back, hop, index, part):
             slot = slots.at[c, lax.rem(z + Z - back, Z), :, part]
@@ -168,8 +168,8 @@
         steps[8] = onward(6, 6, 8, pl.ds(512, 512))
         return steps
 
-    k_steps = gather(kg, ks_sem, kr_sem)
-    q_steps = gather(qg, qs_sem, qr_sem)
+    k_steps = gather(k_hbm, kg, ks_sem, kr_sem)
+    q_steps = gather(q_hbm, qg, qs_sem, qr_sem)
     for d in TWO_HOPS:
         k_steps[d].start()
 
@@ -177,6 +177,9 @@
         slot = kg.at[c, lax.rem(z + Z - d, Z)]
         return remote(slot, slot, kps_sem.at[d], kpr_sem.at[d], partner)
 
+    v_across = remote(v_hbm, v_beside, vs_sem.at[0], vr_sem.at[0], partner)
+    v_across.start()
+    load_k.wait()
     k_partner(0).start()
     for d in (2, 6):
         row = lax.rem(y + d, Y)
@@ -186,7 +189,6 @@
     for load in small_loads:
         load.wait()
     load_q.wait()
-    qg[c, z] = pack(q8)
 
     def last_doc(i):
         return doc_ref[2 * i + 1 : 2 * i + 2, HALF - 1 : HALF].astype(F32)
@@ -262,6 +264,8 @@
         k_steps[d].wait_recv()
         k_partner(d).start()
 
+    for d in TWO_HOPS:
+        q_steps[d].start()
     for d in (1, 3, 2):
         t_copies[d].wait_recv()
     ytag[y] = xtag[X - 1]
@@ -290,8 +294,32 @@
     k_steps[4].wait_recv()
     k_steps[8].wait_recv()
     k_partner(4).start()
-    for d in TWO_HOPS:
-        q_steps[d].start()
+    v_across.wait_recv()
+    end_doc = last_doc(NT - 1)
+    mine = jnp.zeros((LANE, WIDTH), F32)
+    theirs = jnp.zeros((LANE, WIDTH), F32)
+    for a in range(2):
+        keys = kg[c].astype(F32)[:, 8 * a : 8 * a + 8, :]
+        docs = jnp.concatenate([doc_row(8 * a + i) for i in range(8)], axis=1)
+        kept = jnp.where(docs == end_doc, keys.reshape(LANE, 1024), 0.0).astype(BF16)
+        mine = mine + dot(kept, v[a * 1024 : (a + 1) * 1024, :])
+        theirs = theirs + dot(kept, v_beside[a * 1024 : (a + 1) * 1024, :])
+    for p in range(X):
+        tails[p, c] = mine[p * QROWS : (p + 1) * QROWS].astype(BF16)
+        tails[p, 1 - c] = theirs[p * QROWS : (p + 1) * QROWS].astype(BF16)
+
+    x_copies = {}
+    for d in (2, 1, 3):
+        x_copies[d] = remote(
+            tails.at[lax.rem(x + d, X)], xbuf.at[x], xs_sem.at[d], xr_sem.at[d], at_x(d)
+        )
+        x_copies[d].start()
+    xbuf[x] = tails[x]
+    for d, first, second in ((2, 3, 4), (6, 5, 8)):
+        q_steps[d].wait_recv()
+        q_steps[first].start()
+        q_steps[second].start()
+
     for d in (0, 2, 6, 1, 7, 3, 5, 4):
         k_partner(d).wait_recv()
 
@@ -317,27 +345,8 @@
     ]
     for j in range(4):
         left10[j] = pairs[j].astype(BF16)
-    quads = [
-        pairs[2 * j + 1] + same(last_doc(4 * j + 1), last_doc(4 * j + 3)) * pairs[2 * j]
-        for j in range(2)
-    ]
-    left11[...] = quads[0].astype(BF16)
-    tail = quads[1] + same(last_doc(3), last_doc(7)) * quads[0]
-    for p in range(X):
-        tails[p] = tail[p * QROWS : (p + 1) * QROWS].astype(BF16)
-
-    x_copies = {}
-    for d in (2, 1, 3):
-        x_copies[d] = remote(
-            tails.at[lax.rem(x + d, X)], xbuf.at[x], xs_sem.at[d], xr_sem.at[d], at_x(d)
-        )
-        x_copies[d].start()
-    xbuf[x] = tails[x]
-
-    for d, first, second in ((2, 3, 4), (6, 5, 8)):
-        q_steps[d].wait_recv()
-        q_steps[first].start()
-        q_steps[second].start()
+    first_quad = pairs[1] + same(last_doc(1), last_doc(3)) * pairs[0]
+    left11[...] = first_quad.astype(BF16)
 
     for d in (1, 3, 2):
         x_copies[d].wait_recv()
@@ -358,27 +367,33 @@
         def _():
             y_copy(d).start()
 
-    blank = jnp.zeros((QROWS, WIDTH), BF16)
-    xlow[0, :QROWS] = blank
-    xlow[0, QROWS:] = blank
-    xlow[1, :QROWS] = xbuf[0]
-    xlow[1, QROWS:] = blank
-    xlow[2, :QROWS] = blank
-    xlow[2, QROWS:] = low_pair.astype(BF16)
-    xlow[3, :QROWS] = xbuf[2]
-    xlow[3, QROWS:] = low_pair.astype(BF16)
-    a_copies = {}
-    for d in (2, 1, 3):
-        a_copies[d] = remote(
-            xlow.at[lax.rem(x + d, X)], xout.at[x], as_sem.at[d], ar_sem.at[d], at_x(d)
-        )
-        a_copies[d].start()
-    xout[x] = xlow[x]
+    blank = jnp.zeros((2, QROWS, WIDTH), BF16)
+    low = low_pair.astype(BF16)
+    pieces = [(blank, blank), (xbuf[0], blank), (blank, low), (xbuf[2], low)]
+    for p in range(X):
+        for b in range(X_LEVELS):
+            for core in range(2):
+                xlow[p, core, b] = pieces[p][b][core]
+
+    def fan_out(make):
+        return [make(d, d, at_x(d), c) for d in (2, 1, 3)] + [
+            make(d, X + d, beside_x(d), 1 - c) for d in (2, 1, 3, 0)
+        ]
+
+    def a_copy(d, index, device, core):
+        source = xlow.at[lax.rem(x + d, X), core]
+        return remote(source, xout.at[c, x], as_sem.at[index], ar_sem.at[index], device)
+
+    a_copies = fan_out(a_copy)
+    for copy in a_copies:
+        copy.start()
+    xout[c, x] = xlow[x, c]
 
     for d in (1, 7, 3, 5, 4, 8):
         q_steps[d].wait_recv()
     q_partner = remote(qg.at[c], qg.at[c], qps_sem.at[0], qpr_sem.at[0], partner)
     q_partner.start()
+
     q_partner.wait_recv()
 
     def near_tile(i, queries):
@@ -429,15 +444,18 @@
     def y_end(row):
         return ytag[row].astype(F32)[0:1, 0:1]
 
-    def b_copy(b, d):
-        index = b * X + d
-        return remote(ylow.at[b], yout.at[x, b], bs_sem.at[index], br_sem.at[index], at_x(d))
+    def b_copies(b):
+        def b_copy(d, index, device, core):
+            send, recv = bs_sem.at[b * 2 * X + index], br_sem.at[b * 2 * X + index]
+            return remote(ylow.at[b, core], yout.at[c, x, b], send, recv, device)
+
+        return fan_out(b_copy)
 
     def hand_on(b, merged):
         ylow[b] = merged
-        yout[x, b] = merged
-        for d in (2, 1, 3):
-            b_copy(b, d).start()
+        for copy in b_copies(b):
+            copy.start()
+        yout[c, x, b] = ylow[b, c]
 
     bits = [lax.rem(y, 2) == 1, lax.rem(lax.div(y, 2), 2) == 1, y >= 4]
     four = lax.div(y, 4) * 4
@@ -468,12 +486,12 @@
         for a, queries in enumerate(unpacked(qg, j)):
             near_tile(a * (NT // 2) + j, queries)
 
-    for d in (1, 3, 2):
-        a_copies[d].wait_recv()
+    for copy in a_copies:
+        copy.wait_recv()
     before = xtag[jnp.maximum(x - 1, 0)].astype(F32)[0:1, 0:1]
     x_masks = [same(before, first_doc), same(ends[1], first_doc)]
     for b in range(2):
-        rows = xout[:, b * QROWS : (b + 1) * QROWS, :].astype(F32).reshape(HALF, WIDTH)
+        rows = xout[:, :, b].astype(F32).reshape(HALF, WIDTH)
         bx[b * HALF : (b + 1) * HALF] = (rows * x_masks[b]).astype(BF16)
 
     @pl.loop(0, NT // 2)
@@ -486,9 +504,9 @@
 
         @pl.when(bits[b])
         def _():
-            for d in (1, 3, 2):
-                b_copy(b, d).wait_recv()
-            rows = yout[:, b].astype(F32).reshape(HALF, WIDTH)
+            for copy in b_copies(b):
+                copy.wait_recv()
+            rows = yout[:, :, b].astype(F32).reshape(HALF, WIDTH)
             mask = same(y_end(y_ends[b]), first_doc)
             by[b * HALF : (b + 1) * HALF] = (rows * mask).astype(BF16)
 
@@ -498,16 +516,18 @@
     for d in range(Z):
         k_partner(d).wait_send()
     q_partner.wait_send()
+    v_across.wait_send()
     for d in range(1, X):
         t_copies[d].wait_send()
         x_copies[d].wait_send()
-        a_copies[d].wait_send()
+    for copy in a_copies:
+        copy.wait_send()
     for b in range(Y_LEVELS):
 
         @pl.when(bits[b])
         def _():
-            for d in range(1, X):
-                b_copy(b, d).wait_send()
+            for copy in b_copies(b):
+                copy.wait_send()
 
     for d in range(1, Y):
 
@@ -528,14 +548,19 @@
         copy.wait()
 
 
+def folded(shard):
+    tokens, width = shard.shape
+    return shard.T.reshape(width, 2, tokens // 2).swapaxes(0, 1).reshape(2 * width, tokens // 2)
+
+
 def local(queries, key_vectors, values, level_table, level_class, doc_ids):
     tokens, width = values.shape
     vmem = pl.BlockSpec(memory_space=pltpu.VMEM)
     hbm = pl.BlockSpec(memory_space=pltpu.HBM)
     dma = pltpu.SemaphoreType.DMA
     arguments = (
-        key_vectors.T,
-        queries.T,
+        folded(key_vectors),
+        folded(queries),
         values,
         level_table,
         level_class.reshape(tokens // HALF, HALF),
@@ -554,8 +579,7 @@
             pltpu.VMEM(level_table.shape, F32),
             pltpu.VMEM((tokens // HALF, HALF), jnp.int32),
             pltpu.VMEM((tokens // HALF, HALF), jnp.int32),
-            pltpu.VMEM((8, tokens), BF16),
-            pltpu.VMEM((8, tokens), BF16),
+            pltpu.VMEM((tokens, width), BF16),
             pltpu.VMEM((tokens, width), BF16),
             pltpu.VMEM((2, Z, 16, tokens // 2), BF16),
             pltpu.VMEM((2, Z, 16, tokens // 2), BF16),
@@ -567,16 +591,16 @@
             pltpu.VMEM((NT, HALF, WIDTH), BF16),
             pltpu.VMEM((4, HALF, WIDTH), BF16),
             pltpu.VMEM((HALF, WIDTH), BF16),
-            pltpu.VMEM((X, QROWS, WIDTH), BF16),
+            pltpu.VMEM((X, 2, QROWS, WIDTH), BF16),
             pltpu.VMEM((X, TAG, HALF), BF16),
             pltpu.VMEM((Y, TAG, HALF), BF16),
-            pltpu.VMEM((X, QROWS, WIDTH), BF16),
-            pltpu.VMEM((X, 2 * QROWS, WIDTH), BF16),
-            pltpu.VMEM((X, 2 * QROWS, WIDTH), BF16),
-            pltpu.VMEM((QROWS, WIDTH), BF16),
-            pltpu.VMEM((Y, QROWS, WIDTH), BF16),
-            pltpu.VMEM((Y_LEVELS, QROWS, WIDTH), BF16),
-            pltpu.VMEM((X, Y_LEVELS, QROWS, WIDTH), BF16),
+            pltpu.VMEM((X, 2, QROWS, WIDTH), BF16),
+            pltpu.VMEM((X, 2, X_LEVELS, QROWS, WIDTH), BF16),
+            pltpu.VMEM((2, X, X_LEVELS, QROWS, WIDTH), BF16),
+            pltpu.VMEM((2, QROWS, WIDTH), BF16),
+            pltpu.VMEM((Y, 2, QROWS, WIDTH), BF16),
+            pltpu.VMEM((Y_LEVELS, 2, QROWS, WIDTH), BF16),
+            pltpu.VMEM((2, X, Y_LEVELS, QROWS, WIDTH), BF16),
             pltpu.VMEM((X_LEVELS * HALF, WIDTH), BF16),
             pltpu.VMEM((NT, TILE, X_LEVELS * HALF), BF16),
             dma((6,)),
@@ -590,17 +614,19 @@
             dma((1,)),
             dma((X,)),
             dma((X,)),
-            dma((X,)),
-            dma((X,)),
+            dma((2 * X,)),
+            dma((2 * X,)),
             dma((Y,)),
             dma((Y,)),
-            dma((Y_LEVELS * X,)),
-            dma((Y_LEVELS * X,)),
+            dma((Y_LEVELS * 2 * X,)),
+            dma((Y_LEVELS * 2 * X,)),
             dma((X,)),
             dma((X,)),
             dma((Y,)),
             dma((Y,)),
             pltpu.SemaphoreType.REGULAR((2,)),
+            dma((1,)),
+            dma((1,)),
         ],
         compiler_params=pltpu.CompilerParams(
             collective_id=0, has_side_effects=True, vmem_limit_bytes=40 * 1024 * 1024

time: 38.5 us -> 35.9 us (0.932)
  the two profiles are of different devices: /device:TPU:1 before, /device:TPU:57 now
where the time goes in v2:
time: 35.9 us; the launch traced here: 35.7 us
  Pallas kernels  35.6 us (99%)
    pallas_call x1, Pallas kernels, local(): pl.pallas_call(body, out_shape=[pltpu.VMEM((NT, TILE, WIDTH), F32), pltpu...  34.2 us
    pallas_call x1, Pallas kernels, local(): pl.pallas_call(last, out_shape=jax.ShapeDtypeStruct((tokens, width), BF16...  1.49 us

profile of v2, /device:TPU:57, one launch (start us, length us, event | category | flops | bytes accessed | tf_op | source)
XLA Modules:
  0.0 35.7 jit_solution(2547156350383851324)
XLA Ops:
  0.0 34.2 %blocks_and_states.1 = (f32[8,256,256]{2,1,0:T(8,128)S(1)}, bf16[8,256,384]{2,1,0:T(8,128)(2,1)S(1)}, bf16[384,256]{1,0:T(8,128)(2,1)S(1)}) custom-call(bf16[16,1024]{1,0:T(8,128)(2,1)} %bitcast.16, bf16[16,1024]{1,0:T(8,128)(2,1)} %bitcast.17, bf16[2048,256]{1,0:T(8,128)(2,1)} %v_hbm.1, f32[8,17]{1,0:T(8,128)} %tab_hbm.1, s32[16,128]{1,0:T(8,128)} %bitcast.18, ...), custom_call_target="tpu_custom_call" | custom-call | tf_op jit(solution)/shard_map/blocks_and_states/pallas_call | solution.py:569
  34.2 1.5 %rows_before.1 = bf16[2048,256]{1,0:T(8,128)(2,1)} custom-call(f32[8,256,256]{2,1,0:T(8,128)S(1)} %get-tuple-element.8.near, bf16[8,256,384]{2,1,0:T(8,128)(2,1)S(1)} %get-tuple-element.9.qy, bf16[384,256]{1,0:T(8,128)(2,1)S(1)} %get-tuple-element.10.by), custom_call_target="tpu_custom_call" | custom-call | tf_op jit(solution)/shard_map/rows_before/pallas_call | solution.py:636

commit v3 on v2

--- a/solution.py
+++ b/solution.py
@@ -57,6 +57,7 @@
     onehot,
     table,
     grid,
+    scale,
     kt,
     state,
     left9,
@@ -133,7 +134,7 @@
     barrier = pltpu.get_barrier_semaphore()
     peers = [at_z(d) for d in TWO_HOPS] + [at_x(d) for d in (2, 1, 3)]
     peers = peers + [at_y(lax.rem(y + d, Y)) for d in TWO_HOPS]
-    peers = peers + [beside_x(d) for d in (2, 1, 3, 0)]
+    peers = peers + [partner]
     for peer in peers:
         pl.semaphore_signal(barrier, inc=1, device_id=peer, device_id_type=MESH)
 
@@ -249,6 +250,20 @@
                 grid[i, rows, :HALF] = jnp.where(doc_t == doc_row(2 * i), weight, 0.0)
             else:
                 grid[i, rows, HALF:] = jnp.zeros((HALF, HALF), F32)
+        wide = lax.dot_general(
+            onehot[i], table[:, 9 * HALF :], DIM0, preferred_element_type=F32
+        )
+        doc_t = wide[:, :HALF]
+        for b in range(MID_LEVELS + FAR_LEVELS):
+            weight = wide[:, (1 + b) * HALF : (2 + b) * HALF]
+            if b < MID_LEVELS:
+                end = jnp.maximum((i >> b << b) - 1, 0)
+                end_doc = doc_row(2 * end + 1)[:, HALF - 1 : HALF]
+                present = jnp.where((i >> b) % 2 == 1, 1.0, 0.0).astype(F32)
+                weight = jnp.where(doc_t == end_doc, weight * present, 0.0)
+            else:
+                weight = jnp.where(doc_t == first_doc, weight, 0.0)
+            scale[i, :, b * HALF : (b + 1) * HALF] = weight
 
     @pl.loop(0, NT // 2)
     def _(i):
@@ -402,17 +417,9 @@
         scores = dot(turned.astype(BF16), kt[i])
         weighted = (scores * grid[i]).astype(BF16)
         total = dot(weighted, v[rows, :])
-        wide = lax.dot_general(
-            onehot[i], table[:, 9 * HALF :], DIM0, preferred_element_type=F32
-        )
-        doc_t = wide[:, :HALF]
         mids = []
         for b in range(MID_LEVELS):
-            end = jnp.maximum((i >> b << b) - 1, 0)
-            end_doc = doc_row(2 * end + 1)[:, HALF - 1 : HALF]
-            present = jnp.where((i >> b) % 2 == 1, 1.0, 0.0).astype(F32)
-            weight = jnp.where(doc_t == end_doc, wide[:, (1 + b) * HALF : (2 + b) * HALF], 0.0)
-            mids.append((weight * (turned * present)).astype(BF16))
+            mids.append((scale[i, :, b * HALF : (b + 1) * HALF] * turned).astype(BF16))
         lefts = [
             left9[jnp.maximum(i - 1, 0)],
             left10[jnp.maximum((i >> 1) - 1, 0)],
@@ -420,12 +427,11 @@
         ]
         total = total + dot(jnp.concatenate(mids, axis=1), jnp.concatenate(lefts, axis=0))
         near[i] = total
-        kept = jnp.where(doc_t == first_doc, turned, 0.0)
         for b in range(FAR_LEVELS):
-            start = (1 + MID_LEVELS + b) * HALF
+            start = (MID_LEVELS + b) * HALF
             target, place = (qx, b) if b < X_LEVELS else (qy, b - X_LEVELS)
             columns = slice(place * HALF, (place + 1) * HALF)
-            target[i, :, columns] = (wide[:, start : start + HALF] * kept).astype(BF16)
+            target[i, :, columns] = (scale[i, :, start : start + HALF] * turned).astype(BF16)
 
     @pl.loop(0, NT // 4)
     def _(j):
@@ -586,6 +592,7 @@
             pltpu.VMEM((NT, 32, TILE), BF16),
             pltpu.VMEM((32, 18 * HALF), BF16),
             pltpu.VMEM((NT, TILE, TILE), F32),
+            pltpu.VMEM((NT, TILE, (MID_LEVELS + FAR_LEVELS) * HALF), F32),
             pltpu.VMEM((NT, HALF, TILE), BF16),
             pltpu.VMEM((NT, HALF, WIDTH), F32),
             pltpu.VMEM((NT, HALF, WIDTH), BF16),

time: 35.9 us -> 35.6 us (level)
  Pallas kernels: 35.6 us -> 35.2 us
    pallas_call x1, Pallas kernels: 34.2 us -> 33.7 us  [local(): pl.pallas_call(body, out_shape=[pltpu.VMEM((NT, TILE, WIDTH), F32), pltpu...]
where the time goes in v3:
time: 35.6 us; the launch traced here: 35.2 us
  Pallas kernels  35.2 us (99%)
    pallas_call x1, Pallas kernels, local(): pl.pallas_call(body, out_shape=[pltpu.VMEM((NT, TILE, WIDTH), F32), pltpu...  33.7 us
    pallas_call x1, Pallas kernels, local(): pl.pallas_call(last, out_shape=jax.ShapeDtypeStruct((tokens, width), BF16...  1.49 us

profile of v3, /device:TPU:57, one launch (start us, length us, event | category | flops | bytes accessed | tf_op | source)
XLA Modules:
  0.0 35.2 jit_solution(3748023131849849391)
XLA Ops:
  0.0 33.7 %blocks_and_states.1 = (f32[8,256,256]{2,1,0:T(8,128)S(1)}, bf16[8,256,384]{2,1,0:T(8,128)(2,1)S(1)}, bf16[384,256]{1,0:T(8,128)(2,1)S(1)}) custom-call(bf16[16,1024]{1,0:T(8,128)(2,1)} %bitcast.16, bf16[16,1024]{1,0:T(8,128)(2,1)} %bitcast.17, bf16[2048,256]{1,0:T(8,128)(2,1)} %v_hbm.1, f32[8,17]{1,0:T(8,128)} %tab_hbm.1, s32[16,128]{1,0:T(8,128)} %bitcast.18, ...), custom_call_target="tpu_custom_call" | custom-call | tf_op jit(solution)/shard_map/blocks_and_states/pallas_call | solution.py:575
  33.7 1.5 %rows_before.1 = bf16[2048,256]{1,0:T(8,128)(2,1)} custom-call(f32[8,256,256]{2,1,0:T(8,128)S(1)} %get-tuple-element.8.near, bf16[8,256,384]{2,1,0:T(8,128)(2,1)S(1)} %get-tuple-element.9.qy, bf16[384,256]{1,0:T(8,128)(2,1)S(1)} %get-tuple-element.10.by), custom_call_target="tpu_custom_call" | custom-call | tf_op jit(solution)/shard_map/rows_before/pallas_call | solution.py:643

commit v4 on v3

--- a/solution.py
+++ b/solution.py
@@ -169,10 +169,28 @@
         steps[8] = onward(6, 6, 8, pl.ds(512, 512))
         return steps
 
-    k_steps = gather(k_hbm, kg, ks_sem, kr_sem)
+    def half(h):
+        return pl.ds(512 * h, 512)
+
+    def k_own(d, h):
+        slot = kg.at[c, z, :, half(h)]
+        index = 2 * d + h
+        return remote(k_hbm.at[:, half(h)], slot, ks_sem.at[index], kr_sem.at[index], at_z(d))
+
+    def k_onward(back, hop, d, h):
+        slot = kg.at[c, lax.rem(z + Z - back, Z), :, half(h)]
+        index = 2 * d + h
+        return remote(slot, slot, ks_sem.at[index], kr_sem.at[index], at_z(hop))
+
+    k_steps = {(d, h): k_own(d, h) for d in TWO_HOPS for h in range(2)}
+    for h in range(2):
+        k_steps[3, h] = k_onward(2, 1, 3, h)
+        k_steps[5, h] = k_onward(6, 7, 5, h)
+    k_steps[4, 0] = k_onward(2, 2, 4, 0)
+    k_steps[4, 1] = k_onward(6, 6, 4, 1)
     q_steps = gather(q_hbm, qg, qs_sem, qr_sem)
-    for d in TWO_HOPS:
-        k_steps[d].start()
+    for step in ((2, 0), (6, 1), (2, 1), (6, 0), (1, 0), (7, 1), (1, 1), (7, 0)):
+        k_steps[step].start()
 
     def k_partner(d):
         slot = kg.at[c, lax.rem(z + Z - d, Z)]
@@ -269,14 +287,16 @@
     def _(i):
         grid_tile(i)
 
-    for d, first, second in ((2, 3, 4), (6, 5, 8)):
-        k_steps[d].wait_recv()
-        k_steps[first].start()
-        k_steps[second].start()
+    onwards = {(2, 0): [(4, 0), (3, 0)], (6, 1): [(4, 1), (5, 1)], (2, 1): [(3, 1)], (6, 0): [(5, 0)]}
+    for step, following in onwards.items():
+        k_steps[step].wait_recv()
+        for other in following:
+            k_steps[other].start()
     k_partner(2).start()
     k_partner(6).start()
     for d in (1, 7):
-        k_steps[d].wait_recv()
+        for h in range(2):
+            k_steps[d, h].wait_recv()
         k_partner(d).start()
 
     for d in TWO_HOPS:
@@ -303,12 +323,10 @@
 
     by[...] = jnp.zeros_like(by)
     load_v.wait()
-    for d in (3, 5):
-        k_steps[d].wait_recv()
+    for d in (3, 5, 4):
+        for h in range(2):
+            k_steps[d, h].wait_recv()
         k_partner(d).start()
-    k_steps[4].wait_recv()
-    k_steps[8].wait_recv()
-    k_partner(4).start()
     v_across.wait_recv()
     end_doc = last_doc(NT - 1)
     mine = jnp.zeros((LANE, WIDTH), F32)
@@ -518,6 +536,7 @@
 
     for step in k_steps:
         k_steps[step].wait_send()
+    for step in q_steps:
         q_steps[step].wait_send()
     for d in range(Z):
         k_partner(d).wait_send()
@@ -611,8 +630,8 @@
             pltpu.VMEM((X_LEVELS * HALF, WIDTH), BF16),
             pltpu.VMEM((NT, TILE, X_LEVELS * HALF), BF16),
             dma((6,)),
-            dma((Z + 1,)),
-            dma((Z + 1,)),
+            dma((2 * Z,)),
+            dma((2 * Z,)),
             dma((Z,)),
             dma((Z,)),
             dma((Z + 1,)),

time: 35.6 us -> 35.1 us (0.986)
  no operation moved by 1% of the time
where the time goes in v4:
time: 35.1 us; the launch traced here: 35 us
  Pallas kernels  35 us (100%)
    pallas_call x1, Pallas kernels, local(): pl.pallas_call(body, out_shape=[pltpu.VMEM((NT, TILE, WIDTH), F32), pltpu...  33.5 us
    pallas_call x1, Pallas kernels, local(): pl.pallas_call(last, out_shape=jax.ShapeDtypeStruct((tokens, width), BF16...  1.49 us

profile of v4, /device:TPU:57, one launch (start us, length us, event | category | flops | bytes accessed | tf_op | source)
XLA Modules:
  0.0 35.0 jit_solution(9362146942893105370)
XLA Ops:
  0.0 33.5 %blocks_and_states.1 = (f32[8,256,256]{2,1,0:T(8,128)S(1)}, bf16[8,256,384]{2,1,0:T(8,128)(2,1)S(1)}, bf16[384,256]{1,0:T(8,128)(2,1)S(1)}) custom-call(bf16[16,1024]{1,0:T(8,128)(2,1)} %bitcast.16, bf16[16,1024]{1,0:T(8,128)(2,1)} %bitcast.17, bf16[2048,256]{1,0:T(8,128)(2,1)} %v_hbm.1, f32[8,17]{1,0:T(8,128)} %tab_hbm.1, s32[16,128]{1,0:T(8,128)} %bitcast.18, ...), custom_call_target="tpu_custom_call" | custom-call | tf_op jit(solution)/shard_map/blocks_and_states/pallas_call | solution.py:594
  33.5 1.5 %rows_before.1 = bf16[2048,256]{1,0:T(8,128)(2,1)} custom-call(f32[8,256,256]{2,1,0:T(8,128)S(1)} %get-tuple-element.8.near, bf16[8,256,384]{2,1,0:T(8,128)(2,1)S(1)} %get-tuple-element.9.qy, bf16[384,256]{1,0:T(8,128)(2,1)S(1)} %get-tuple-element.10.by), custom_call_target="tpu_custom_call" | custom-call | tf_op jit(solution)/shard_map/rows_before/pallas_call | solution.py:662

commit v5 on v4

--- a/solution.py
+++ b/solution.py
@@ -505,11 +505,6 @@
         merged = late + same(y_end(1), y_end(3)) * early
         hand_on(2, merged.astype(BF16))
 
-    @pl.loop(NT // 4, NT // 2)
-    def _(j):
-        for a, queries in enumerate(unpacked(qg, j)):
-            near_tile(a * (NT // 2) + j, queries)
-
     for copy in a_copies:
         copy.wait_recv()
     before = xtag[jnp.maximum(x - 1, 0)].astype(F32)[0:1, 0:1]
@@ -518,10 +513,12 @@
         rows = xout[:, :, b].astype(F32).reshape(HALF, WIDTH)
         bx[b * HALF : (b + 1) * HALF] = (rows * x_masks[b]).astype(BF16)
 
-    @pl.loop(0, NT // 2)
+    @pl.loop(NT // 4, NT // 2)
     def _(j):
-        for i in (2 * j, 2 * j + 1):
-            near[i] = near[i] + dot(qx[i], bx[...])
+        for a, queries in enumerate(unpacked(qg, j)):
+            near_tile(a * (NT // 2) + j, queries)
+        for done in (j - NT // 4, j + NT // 4, j, j + NT // 2):
+            near[done] = near[done] + dot(qx[done], bx[...])
 
     y_ends = [y - 1, four + 1, 3]
     for b in range(Y_LEVELS):

time: 35.1 us -> 35.1 us (level)
  no operation moved by 1% of the time
where the time goes in v5:
time: 35.1 us; the launch traced here: 35 us
  Pallas kernels  35 us (100%)
    pallas_call x1, Pallas kernels, local(): pl.pallas_call(body, out_shape=[pltpu.VMEM((NT, TILE, WIDTH), F32), pltpu...  33.5 us
    pallas_call x1, Pallas kernels, local(): pl.pallas_call(last, out_shape=jax.ShapeDtypeStruct((tokens, width), BF16...  1.49 us

profile of v5, /device:TPU:57, one launch (start us, length us, event | category | flops | bytes accessed | tf_op | source)
XLA Modules:
  0.0 35.0 jit_solution(1594057709536485444)
XLA Ops:
  0.0 33.5 %blocks_and_states.1 = (f32[8,256,256]{2,1,0:T(8,128)S(1)}, bf16[8,256,384]{2,1,0:T(8,128)(2,1)S(1)}, bf16[384,256]{1,0:T(8,128)(2,1)S(1)}) custom-call(bf16[16,1024]{1,0:T(8,128)(2,1)} %bitcast.16, bf16[16,1024]{1,0:T(8,128)(2,1)} %bitcast.17, bf16[2048,256]{1,0:T(8,128)(2,1)} %v_hbm.1, f32[8,17]{1,0:T(8,128)} %tab_hbm.1, s32[16,128]{1,0:T(8,128)} %bitcast.18, ...), custom_call_target="tpu_custom_call" | custom-call | tf_op jit(solution)/shard_map/blocks_and_states/pallas_call | solution.py:591
  33.5 1.5 %rows_before.1 = bf16[2048,256]{1,0:T(8,128)(2,1)} custom-call(f32[8,256,256]{2,1,0:T(8,128)S(1)} %get-tuple-element.8.near, bf16[8,256,384]{2,1,0:T(8,128)(2,1)S(1)} %get-tuple-element.9.qy, bf16[384,256]{1,0:T(8,128)(2,1)S(1)} %get-tuple-element.10.by), custom_call_target="tpu_custom_call" | custom-call | tf_op jit(solution)/shard_map/rows_before/pallas_call | solution.py:659
